TPU v7x, 768 devices: a whole 4x8x12 slice. The times are simulated.
768 devices in a mesh: diag: 32 (over x_lo, y, core), off: 24 (over x_hi, z).
Axes of the slice: x: 4 (x_hi: 2, x_lo: 2; x = x_hi * 2 + x_lo), y: 8, z: 12, core: 2. Of those that a mesh axis runs over, the one named last changes fastest.
Arguments:
- vectors: bfloat16 [16, 98304], P(None, ('diag', 'off')), may hold values from -6 to 6
- tiles: bfloat16 [32, 24, 32, 128, 128], P('diag', 'off'), may hold values from -0.0625 to 0.0625
- row_index: int32 [32, 24, 32], P('diag', 'off'), may hold values from 0 to 23
- col_index: int32 [32, 24, 32], P('diag', 'off'), may hold values from 0 to 23
- counts: int32 [32, 24], P('diag', 'off'), may hold values from 8 to 32, as said below
Outputs:
- applied: float32 [16, 98304], P(None, ('diag', 'off'))
Inputs may be any that keep to these rules, and one draw needn't show every extreme that they name: `counts`: each cell has 8 to 32 live slots, at the front; some cell has exactly 32.
All inputs are finite; a program needn't handle non-finite values.
Results may differ from a plain program's by a relative error of at most 0.0003.
Values may be sent and summed in bfloat16 or wider, within the bound.
A program may use at most 32 MiB of HBM per device.

v0:
```python
import jax
import jax.numpy as jnp
from jax import lax
from jax.sharding import PartitionSpec as P


def column_shift(offset, groups, offsets):
    spread = (offset * groups + offsets - 1) // offsets
    return jnp.where(offset == offsets - 1, groups - 1, spread)


def body(vectors, tiles, row_index, col_index, counts):
    groups = lax.axis_size("diag")
    offsets = lax.axis_size("off")
    my_group = lax.axis_index("diag")
    nvec, piece = vectors.shape
    width = piece * offsets
    tile_size = tiles.shape[-1]
    blocks = width // tile_size
    targets = (
        my_group + column_shift(jnp.arange(offsets, dtype=jnp.int32), groups, offsets)
    ) % groups
    my_offset = lax.axis_index("off")
    partner = (my_group + column_shift(my_offset, groups, offsets)) % groups
    everything = lax.all_gather(vectors, ("diag", "off"), axis=1, tiled=True)
    row_vec = lax.dynamic_slice_in_dim(everything, my_group * width, width, 1)
    col_vec = lax.dynamic_slice_in_dim(everything, partner * width, width, 1)
    batch = tiles[0, 0]
    rows = row_index[0, 0]
    cols = col_index[0, 0]
    live = counts[0, 0]
    row_block = row_vec.reshape(nvec, blocks, tile_size)
    col_block = col_vec.reshape(nvec, blocks, tile_size)
    picked_col = jnp.take(col_block, cols, axis=1)
    picked_row = jnp.take(row_block, rows, axis=1)
    forward = jnp.einsum("vpb,pab->vpa", picked_col, batch, preferred_element_type=jnp.float32)
    backward = jnp.einsum("vpa,pab->vpb", picked_row, batch, preferred_element_type=jnp.float32)
    valid = (jnp.arange(rows.shape[0], dtype=jnp.int32) < live).astype(jnp.float32)
    block_ids = jnp.arange(blocks, dtype=jnp.int32)
    rows_hot = (rows[:, None] == block_ids[None, :]).astype(jnp.float32) * valid[:, None]
    cols_hot = (cols[:, None] == block_ids[None, :]).astype(jnp.float32) * valid[:, None]
    row_part = jnp.einsum(
        "pt,vpa->vta", rows_hot, forward, precision=lax.Precision.HIGHEST
    ).reshape(nvec, width)
    col_part = jnp.einsum(
        "pt,vpb->vtb", cols_hot, backward, precision=lax.Precision.HIGHEST
    ).reshape(nvec, width)
    send_rows = row_part.reshape(nvec, offsets, piece).transpose(1, 0, 2)
    send_cols = col_part.reshape(nvec, offsets, piece).transpose(1, 0, 2)
    back_rows, back_cols = (
        lax.all_to_all(send_rows, "off", split_axis=0, concat_axis=0, tiled=True),
        lax.all_to_all(send_cols, "off", split_axis=0, concat_axis=0, tiled=True),
    )
    owner_hot = (targets[:, None] == jnp.arange(groups, dtype=jnp.int32)[None, :]).astype(
        jnp.float32
    )
    placed = jnp.einsum("kg,kvp->vgp", owner_hot, back_cols, precision=lax.Precision.HIGHEST)
    own_slot = (jnp.arange(groups, dtype=jnp.int32) == my_group).astype(jnp.float32)
    placed = placed + own_slot[None, :, None] * jnp.sum(back_rows, axis=0)[:, None, :]
    placed = placed.reshape(nvec, groups * piece)
    return lax.psum_scatter(placed, "diag", scatter_dimension=1, tiled=True)


def solution(mesh):
    return jax.shard_map(
        body,
        mesh=mesh,
        in_specs=(
            P(None, ("diag", "off")),
            P("diag", "off", None, None, None),
            P("diag", "off", None),
            P("diag", "off", None),
            P("diag", "off"),
        ),
        out_specs=P(None, ("diag", "off")),
        check_vma=False,
    )
```

profile of v0, /device:TPU:6, one launch (start us, length us, event | category | flops | bytes accessed | tf_op | source)
XLA Modules:
  0.0 1765.8 jit_solution(2608126601113353321)
XLA Ops:
  6.5 0.0 copy-start
  6.5 0.0 copy-start.1
  6.5 0.0 all-gather.2.cloned.1.call-start
  6.5 0.7 all-gather.2.cloned.1.call-update
  8.0 0.7 compare_select_fusion
  8.6 0.7 compare_and_fusion
  9.3 0.7 compare_select_fusion.1
  10.0 0.7 compare_and_fusion.1
  10.6 1581.7 %all-gather.2.cloned.1.call-done = bf16[16,98304]{1,0:T(8,128)(2,1)} async-done(((bf16[16,128]{1,0:T(8,128)(2,1)}), bf16[16,98304]{1,0:T(8,128)(2,1)}) %all-gather.2.cloned.1.call-update) | async-done | bytes 3145744 | tf_op jit(solution)/shard_map/all_gather | solution.py:25
  1592.4 1.0 dynamic-slice_bitcast_fusion
  1593.4 0.6 gather_fusion.1
  1594.0 0.0 copy-done
  1594.0 0.7 convolution_bitcast_fusion.1
  1594.7 1.0 fusion.3
  1595.7 0.7 copy.16
  1596.4 11.7 all-to-all-start.1
  1608.1 0.6 gather_fusion
  1608.7 0.4 convolution_bitcast_fusion.2
  1609.2 0.0 copy-done.1
  1609.2 0.4 fusion.5
  1609.6 0.7 copy.12
  1610.3 12.3 all-to-all-done.1
  1622.6 6.6 all-to-all-start
  1629.2 0.0 reduce-scatter.2.cloned.1.call-start
  1629.3 13.4 all-to-all-done
  1642.7 0.4 fusion
  1643.1 0.8 copy.29
  1643.9 0.0 reduce-scatter.2.cloned.1.call-update
  1644.0 115.0 %reduce-scatter.2.cloned.1.call-done = f32[16,128]{1,0:T(8,128)} async-done(((f32[16,4096]{1,0:T(8,128)}), f32[16,128]{1,0:T(8,128)}) %reduce-scatter.2.cloned.1.call-update) | async-done | bytes 8208 | tf_op jit(solution)/shard_map/reduce_scatter | solution.py:61
  (7 shorter events, 0.1 us)
Async XLA Ops:
  6.5 1587.4 %copy-start = (bf16[1,1,32,128,128]{4,3,2,1,0:T(8,128)(2,1)S(1)}, bf16[1,1,32,128,128]{4,3,2,1,0:T(8,128)(2,1)}, u32[]{:S(2)}) copy-start(bf16[1,1,32,128,128]{4,3,2,1,0:T(8,128)(2,1)} %param.8) | copy-start | bytes 3145732
  6.5 1602.6 %copy-start.1 = (s32[1,1,32]{2,1,0:T(1,128)S(1)}, s32[1,1,32]{2,1,0:T(1,128)}, u32[]{:S(2)}) copy-start(s32[1,1,32]{2,1,0:T(1,128)} %param.10) | copy-start | bytes 388
  6.5 1585.8 %all-gather.2.cloned.1.call-start = ((), (), s32[]{:S(2)}) async-start(), calls=%async_computation.3 | async-start | bytes 3149824 | tf_op jit(solution)/shard_map/all_gather | solution.py:25
  1596.4 26.2 %all-to-all-start.1 = ((f32[24,16,128]{2,1,0:T(8,128)}), f32[24,16,128]{2,1,0:T(8,128)S(1)}, u32[]{:S(2)}, u32[]{:S(2)}) async-start(f32[24,16,128]{2,1,0:T(8,128)} %copy.16), calls=%async_computation.1 | async-start | bytes 393216 | tf_op jit(solution)/shard_map/all_to_all | solution.py:51
  1622.6 20.1 %all-to-all-start = ((f32[24,16,128]{2,1,0:T(8,128)}), f32[24,16,128]{2,1,0:T(8,128)S(1)}, u32[]{:S(2)}, u32[]{:S(2)}) async-start(f32[24,16,128]{2,1,0:T(8,128)} %copy.12), calls=%async_computation | async-start | bytes 393216 | tf_op jit(solution)/shard_map/all_to_all | solution.py:52
  1629.2 129.8 %reduce-scatter.2.cloned.1.call-start = ((), (), s32[]{:S(2)}) async-start(), calls=%async_computation.4 | async-start | bytes 270336 | tf_op jit(solution)/shard_map/reduce_scatter | solution.py:61
Sparse Core Ops, SparseCore 0:
  9.9 1582.4 all-gather.1
  1644.1 114.8 reduce-scatter.1
where the time goes:
time: 1770 us
  waiting for transfers between devices  1720 us (97%)
  starting transfers between devices  18.4 us (1%)
    all_gather x1, waiting for transfers between devices, body(): everything = lax.all_gather(vectors, ('diag', 'off'), axis=1, tiled=True)  1580 us
    reduce_scatter x1, waiting for transfers between devices, body(): return lax.psum_scatter(placed, 'diag', scatter_dimension=1, tiled=True)  115 us
  transfers between devices with their start and end apart: 4, of which 4 were waited for; matrix products, arithmetic and copies ran while one was open for 0% of the time, Pallas kernels for 0%

commit v1 on v0

v1 whole, which is shorter than its diff:
```python
import functools

import jax
import jax.numpy as jnp
from jax import lax
from jax.experimental import pallas as pl
from jax.experimental.pallas import tpu as pltpu
from jax.sharding import PartitionSpec as P

MESH = pl.DeviceIdType.MESH
GROUPS = 32
OFFS = 24
RING = 12
SLOTS = 32


def shift(k):
    return lax.div(k * GROUPS + (OFFS - 1), OFFS)


def peer_steps():
    steps = [(f, d) for f in (0, 1) for d in range(RING)]
    hops = lambda s: 2 * s[0] + min(s[1], RING - s[1])
    return sorted(steps, key=lambda s: (-hops(s), s[1] > RING // 2, s))


STEPS = peer_steps()
AWAY = STEPS[:-1]
N_AWAY = len(AWAY)


def kernel(
    vec, tiles_hbm, row_s, col_s, cnt_s, out,
    tiles, tiles_t, rowv, colv, acc, row_out, col_out, row_in, col_in,
    chain, last,
    tile_sem, send_sem, recv_sem,
):
    i = lax.axis_index("diag")
    k = lax.axis_index("off")
    xh = lax.div(k, RING)
    z = lax.rem(k, RING)
    j = lax.rem(i + shift(k), GROUPS)
    away = k != 0

    def member(step):
        flip, dz = step
        h = 1 - xh if flip else xh
        return h * RING + lax.rem(z + dz, RING)

    def user(t):
        return lax.rem(i - shift(t) + GROUPS, GROUPS)

    barrier = pltpu.get_barrier_semaphore()

    def greet(d, o):
        pl.semaphore_signal(barrier, inc=1, device_id=(d, o), device_id_type=MESH)

    for step in AWAY:
        t = member(step)
        greet(j, t)
        greet(i, t)

    @pl.when(away)
    def _():
        greet(j, k)

    load = pltpu.make_async_copy(tiles_hbm.at[0, 0], tiles, tile_sem)
    load.start()

    rowv[k] = vec[...]

    @pl.when(jnp.logical_not(away))
    def _():
        colv[k] = vec[...]

    acc[SLOTS] = jnp.zeros(acc.shape[1:], jnp.float32)

    pl.semaphore_wait(barrier, 2 * N_AWAY + jnp.where(away, 1, 0))

    def send(src, dst, d, o, sem):
        pltpu.make_async_remote_copy(
            src_ref=src, dst_ref=dst, send_sem=send_sem.at[sem], recv_sem=recv_sem.at[sem],
            device_id=(d, o), device_id_type=MESH,
        ).start()

    def wait(ref, n, sem):
        part = ref.at[pl.ds(0, n)]
        pltpu.make_async_copy(part, part, sem).wait()

    for step in AWAY:
        t = member(step)
        send(vec, colv.at[k], user(t), t, 1)
        send(vec, rowv.at[k], i, t, 0)

    @pl.when(away)
    def _():
        send(vec, colv.at[k], user(k), k, 2)

    live = cnt_s[0, 0]
    rows = [row_s[0, 0, q] for q in range(SLOTS)]
    cols = [col_s[0, 0, q] for q in range(SLOTS)]

    def link(p, _):
        r = row_s[0, 0, p]
        c = col_s[0, 0, p]
        before_r = before_c = jnp.int32(SLOTS)
        for q in range(SLOTS):
            earlier = q < p
            before_r = jnp.where(jnp.logical_and(rows[q] == r, earlier), q, before_r)
            before_c = jnp.where(jnp.logical_and(cols[q] == c, earlier), q, before_c)
        chain[p] = before_r
        chain[SLOTS + p] = before_c
        return 0

    lax.fori_loop(0, SLOTS, link, 0)

    def ends(t, _):
        end_r = end_c = jnp.int32(SLOTS)
        for q in range(SLOTS):
            alive = q < live
            end_r = jnp.where(jnp.logical_and(rows[q] == t, alive), q, end_r)
            end_c = jnp.where(jnp.logical_and(cols[q] == t, alive), q, end_c)
        last[t] = end_r
        last[OFFS + t] = end_c
        return 0

    lax.fori_loop(0, OFFS, ends, 0)

    load.wait()

    def flip(p, _):
        tiles_t[p] = tiles[p].T
        return 0

    lax.fori_loop(0, SLOTS, flip, 0)

    def multiply(picked, idx, mats, base):
        def some(block, _):
            for u in range(8):
                p = block * 8 + u
                x = picked[idx[0, 0, p]]
                y = jnp.dot(x, mats[p], preferred_element_type=jnp.float32)
                acc[p] = acc[chain[base + p]] + y
            return 0

        lax.fori_loop(0, SLOTS // 8, some, 0)

    def settle(part, base):
        for t in range(OFFS):
            part[t] = acc[last[base + t]]

    wait(rowv, N_AWAY, recv_sem.at[0])
    multiply(rowv, row_s, tiles, SLOTS)
    settle(col_out, OFFS)

    wait(colv, N_AWAY, recv_sem.at[1])

    @pl.when(away)
    def _():
        wait(colv, 1, recv_sem.at[2])

    for step in AWAY:
        t = member(step)
        send(col_out.at[t], col_in.at[k], j, t, 4)

    @pl.when(away)
    def _():
        send(col_out.at[k], col_in.at[k], j, k, 5)

    multiply(colv, col_s, tiles_t, 0)
    settle(row_out, 0)
    for step in AWAY:
        t = member(step)
        send(row_out.at[t], row_in.at[k], i, t, 3)
    row_in[k] = row_out[k]

    @pl.when(jnp.logical_not(away))
    def _():
        col_in[k] = col_out[k]

    def total(ref):
        s = ref[0]
        for t in range(1, OFFS):
            s = s + ref[t]
        return s

    wait(col_in, N_AWAY, recv_sem.at[4])

    @pl.when(away)
    def _():
        wait(col_in, 1, recv_sem.at[5])

    cols_sum = total(col_in)
    wait(row_in, N_AWAY, recv_sem.at[3])
    out[...] = cols_sum + total(row_in)

    for sem, ref in ((0, rowv), (1, colv), (3, row_out), (4, col_out)):
        wait(ref, N_AWAY, send_sem.at[sem])

    @pl.when(away)
    def _():
        wait(colv, 1, send_sem.at[2])
        wait(col_out, 1, send_sem.at[5])


def body(vectors, tiles, row_index, col_index, counts):
    nvec, piece = vectors.shape
    smem = pl.BlockSpec(memory_space=pltpu.SMEM)
    vmem = pl.BlockSpec(memory_space=pltpu.VMEM)
    block = (nvec, piece)
    return pl.pallas_call(
        kernel,
        out_shape=jax.ShapeDtypeStruct(block, jnp.float32),
        in_specs=[vmem, pl.BlockSpec(memory_space=pl.ANY), smem, smem, smem],
        out_specs=vmem,
        scratch_shapes=[
            pltpu.VMEM(tiles.shape[2:], tiles.dtype),
            pltpu.VMEM(tiles.shape[2:], tiles.dtype),
            pltpu.VMEM((OFFS,) + block, vectors.dtype),
            pltpu.VMEM((OFFS,) + block, vectors.dtype),
            pltpu.VMEM((SLOTS + 1,) + block, jnp.float32),
            pltpu.VMEM((OFFS,) + block, jnp.float32),
            pltpu.VMEM((OFFS,) + block, jnp.float32),
            pltpu.VMEM((OFFS,) + block, jnp.float32),
            pltpu.VMEM((OFFS,) + block, jnp.float32),
            pltpu.SMEM((2 * SLOTS,), jnp.int32),
            pltpu.SMEM((2 * OFFS,), jnp.int32),
            pltpu.SemaphoreType.DMA,
            pltpu.SemaphoreType.DMA((6,)),
            pltpu.SemaphoreType.DMA((6,)),
        ],
        compiler_params=pltpu.CompilerParams(
            collective_id=0, has_side_effects=True, vmem_limit_bytes=24 * 1024 * 1024
        ),
        cost_estimate=pl.CostEstimate(flops=4 * SLOTS * nvec * piece * piece, bytes_accessed=2 * SLOTS * piece * piece, transcendentals=0),
    )(vectors, tiles, row_index, col_index, counts)


def solution(mesh):
    return jax.shard_map(
        body,
        mesh=mesh,
        in_specs=(
            P(None, ("diag", "off")),
            P("diag", "off", None, None, None),
            P("diag", "off", None),
            P("diag", "off", None),
            P("diag", "off"),
        ),
        out_specs=P(None, ("diag", "off")),
        check_vma=False,
    )
```

time: 1770 us -> 51.1 us (0.03)
  the two profiles are of different devices: /device:TPU:6 before, /device:TPU:1 now
where the time goes in v1:
time: 51.1 us; the launch traced here: 50.9 us
  Pallas kernels  47.6 us (93%)
  local copies, waits for them, and re-layouts  2.51 us (5%)
  between operations  0.71 us (1%)
    pallas_call x1, Pallas kernels, body(): pl.pallas_call(kernel, out_shape=jax.ShapeDtypeStruct(block, jnp.float32)...  47.6 us
    unnamed x9, local copies, waits for them, and re-layouts  2.51 us

profile of v1, /device:TPU:1, one launch (start us, length us, event | category | flops | bytes accessed | tf_op | source)
XLA Modules:
  0.0 50.9 jit_solution(14238023162504207044)
XLA Ops:
  0.0 0.0 copy-start.3
  0.0 0.0 copy-start.2
  0.7 0.0 copy-done.3
  0.7 0.0 copy-done.2
  0.7 0.0 copy-start
  0.7 1.2 %copy-done = bf16[1,1,32,128,128]{4,3,2,1,0:T(8,128)(2,1)S(1)} copy-done((bf16[1,1,32,128,128]{4,3,2,1,0:T(8,128)(2,1)S(1)}, bf16[1,1,32,128,128]{4,3,2,1,0:T(8,128)(2,1)}, u32[]{:S(2)}) %copy-start) | copy-done | bytes 1048600
  1.9 0.0 copy-start.1
  1.9 0.7 %copy-done.1 = bf16[16,128]{1,0:T(8,128)(2,1)S(1)} copy-done((bf16[16,128]{1,0:T(8,128)(2,1)S(1)}, bf16[16,128]{1,0:T(8,128)(2,1)}, u32[]{:S(2)}) %copy-start.1) | copy-done | bytes 4120
  2.6 47.6 %shard_map.55 = f32[16,128]{1,0:T(8,128)S(1)} custom-call(bf16[16,128]{1,0:T(8,128)(2,1)S(1)} %copy-done.1, bf16[1,1,32,128,128]{4,3,2,1,0:T(8,128)(2,1)S(1)} %copy-done, s32[1,1,32]{2,1,0:T(1,128)S(1)} %copy-done.2, s32[1,1,32]{2,1,0:T(1,128)S(1)} %copy-done.3, s32[1,1]{1,0:T(1,128)S(6)} %copy.7.cnt_s), custom_call_target="tpu_custom_call" | custom-call | flops 33554432 | bytes 1048576 | tf_op jit(solution)/shard_map/pallas_call | solution.py:211
  50.3 0.6 %copy.8 = f32[16,128]{1,0:T(8,128)} copy(f32[16,128]{1,0:T(8,128)S(1)} %shard_map.55) | data formatting | bytes 16384
Async XLA Ops:
  0.0 0.7 %copy-start.3 = (s32[1,1,32]{2,1,0:T(1,128)S(1)}, s32[1,1,32]{2,1,0:T(1,128)}, u32[]{:S(2)}) copy-start(s32[1,1,32]{2,1,0:T(1,128)} %col_s.1) | copy-start | bytes 388
  0.0 0.7 %copy-start.2 = (s32[1,1,32]{2,1,0:T(1,128)S(1)}, s32[1,1,32]{2,1,0:T(1,128)}, u32[]{:S(2)}) copy-start(s32[1,1,32]{2,1,0:T(1,128)} %row_s.1) | copy-start | bytes 388
  0.7 1.2 %copy-start = (bf16[1,1,32,128,128]{4,3,2,1,0:T(8,128)(2,1)S(1)}, bf16[1,1,32,128,128]{4,3,2,1,0:T(8,128)(2,1)}, u32[]{:S(2)}) copy-start(bf16[1,1,32,128,128]{4,3,2,1,0:T(8,128)(2,1)} %tiles_hbm.1) | copy-start | bytes 3145732
  1.9 0.7 %copy-start.1 = (bf16[16,128]{1,0:T(8,128)(2,1)S(1)}, bf16[16,128]{1,0:T(8,128)(2,1)}, u32[]{:S(2)}) copy-start(bf16[16,128]{1,0:T(8,128)(2,1)} %vec.1) | copy-start | bytes 12292

commit v2 on v0

v2 whole, which is shorter than its diff:
```python
import jax
import jax.numpy as jnp
from jax import lax
from jax.experimental import pallas as pl
from jax.experimental.pallas import tpu as pltpu
from jax.sharding import PartitionSpec as P

MESH = pl.DeviceIdType.MESH
GROUPS, OFFS, RING, SLOTS = 32, 24, 12, 32
NEAR=7
def shift(k): return lax.div(k * GROUPS + (OFFS - 1), OFFS)
N_AWAY=OFFS-1
UP=[h*RING+z for z in range(RING) for h in (0,1)]
LINE=[6,5,7,4,8,3,9,2,10,1,11]
def slot(d): return 0 if d==0 else (2*d-1 if d<=RING//2 else 2*(RING-d))
def kernel(vec_h, tiles_h, row_h, col_h, cnt_h, out,
    tiles, tiles_t, rowv, colv, acc, row_out, col_out, row_in, col_in,
    row_s, col_s, cnt_s, chain, last, place, in_sem, send_sem, recv_sem, ready):
    i = lax.axis_index("diag"); k = lax.axis_index("off")
    xh = lax.div(k, RING); z = lax.rem(k, RING)
    j = lax.rem(i + shift(k), GROUPS)
    U=8
    base = xh * RING
    xk=(1-xh)*RING+z
    away = k!=0
    def user(t): return lax.rem(i - shift(jnp.int32(t)) + GROUPS, GROUPS)
    def line(dz): return base + lax.rem(z + dz, RING)
    barrier = pltpu.get_barrier_semaphore()
    def greet(d, o): pl.semaphore_signal(barrier, inc=1, device_id=(d, o), device_id_type=MESH)
    for dz in LINE[:5]: greet(i,line(dz))
    greet(j, xk)
    @pl.when(away)
    def _(): greet(j, k)
    for dz in LINE[5:]: greet(i,line(dz))
    greet(i, xk)
    loads = [pltpu.make_async_copy(a, b, in_sem.at[n]) for n, (a, b) in enumerate(((vec_h, rowv.at[base]), (row_h, row_s), (col_h, col_s), (cnt_h, cnt_s), (tiles_h.at[0, 0], tiles)))]
    for l in loads: l.start()
    acc[SLOTS] = jnp.zeros(acc.shape[1:], jnp.float32)
    loads[0].wait()
    def prework1():
        for l in loads[1:4]: l.wait()
        live = cnt_s[0, 0]
        rows = [row_s[0, 0, q] for q in range(SLOTS)]
        cols = [col_s[0, 0, q] for q in range(SLOTS)]
        def where_lies(t):
            h=lax.div(t,RING)
            d=lax.rem(lax.rem(t,RING)-z+RING,RING)
            return h*RING+jnp.where(d==0,0,jnp.where(d<=RING//2,2*d-1,2*(RING-d)))
        def link(p, _):
            r = row_s[0, 0, p]; c = col_s[0, 0, p]
            place[p]=where_lies(r); place[SLOTS+p]=where_lies(c)
            before_r = before_c = jnp.int32(SLOTS)
            for q in range(SLOTS):
                earlier = q < p
                before_r = jnp.where(jnp.logical_and(rows[q] == r, earlier), q, before_r)
                before_c = jnp.where(jnp.logical_and(cols[q] == c, earlier), q, before_c)
            chain[p] = before_r; chain[SLOTS + p] = before_c
            return 0
        lax.fori_loop(0, SLOTS, link, 0)
        def ends(t, _):
            end_r = end_c = jnp.int32(SLOTS)
            for q in range(SLOTS):
                alive = q < live
                end_r = jnp.where(jnp.logical_and(rows[q] == t, alive), q, end_r)
                end_c = jnp.where(jnp.logical_and(cols[q] == t, alive), q, end_c)
            last[t] = end_r; last[OFFS + t] = end_c
            return 0
        lax.fori_loop(0, OFFS, ends, 0)
    def prework2():
        loads[4].wait()
        def flip(p, _):
            tiles_t[p] = tiles[p].T
            return 0
        lax.fori_loop(0, SLOTS, flip, 0)
    pre=(1, 2)
    if pre[0]==0: prework1()
    if pre[1]==0: prework2()
    pl.semaphore_wait(barrier, len(LINE) + 2 + jnp.where(away, 1, 0))
    def send(src, dst, d, o, sem, rsem=None):
        pltpu.make_async_remote_copy(src_ref=src, dst_ref=dst, send_sem=send_sem.at[sem], recv_sem=recv_sem.at[sem if rsem is None else rsem], device_id=(d, o), device_id_type=MESH).start()
    def wait(ref, n, sem):
        part = ref.at[pl.ds(0, n)]
        pltpu.make_async_copy(part, part, sem).wait()
    mine = rowv.at[base]
    for dz in LINE:
        s=slot((RING-dz)%RING)
        send(mine, rowv.at[base+s], i, line(dz), 0 if s<NEAR else 1)
    pl.semaphore_signal(ready, inc=1, device_id=(user(xk), xk), device_id_type=MESH)
    @pl.when(away)
    def _(): pl.semaphore_signal(ready, inc=1, device_id=(user(k), k), device_id_type=MESH)
    if pre[0]==1: prework1()
    if pre[1]==1: prework2()
    def pass_on(first,n,f):
        part=pl.ds(base+first,n)
        send(rowv.at[part], colv.at[part], user(xk), xk, 2+2*f, 2+2*f+xh)
        @pl.when(away)
        def _(): send(rowv.at[part], colv.at[part], user(k), k, 3+2*f, 2+2*f+xh)
        send(rowv.at[part], rowv.at[part], i, xk, 6+f)
    wait(rowv, NEAR-1, recv_sem.at[0])
    pass_on(0,NEAR,0)
    wait(rowv, RING-NEAR, recv_sem.at[1])
    pass_on(NEAR,RING-NEAR,1)
    @pl.when(jnp.logical_not(away))
    def _(): colv[pl.ds(base,RING)] = rowv[pl.ds(base,RING)]
    if pre[0]==2: prework1()
    if pre[1]==2: prework2()
    def multiply(picked, at, mats, base):
        def some(block, _):
            for u in range(U):
                p = block * U + u
                x = picked[place[at+p]]
                y = jnp.dot(x, mats[p], preferred_element_type=jnp.float32)
                acc[p] = acc[chain[base + p]] + y
            return 0
        if U==SLOTS: some(0,0)
        else: lax.fori_loop(0, SLOTS // U, some, 0)
    wait(rowv, NEAR, recv_sem.at[6])
    wait(rowv, RING-NEAR, recv_sem.at[7])
    multiply(rowv, 0, tiles, SLOTS)
    for t in range(OFFS): col_out[t] = acc[last[OFFS + t]]
    pl.semaphore_wait(ready, 1 + jnp.where(away, 1, 0))
    for t in UP:
        def go(t=t): send(col_out.at[t], col_in.at[k], j, t, 8)
        if t==0: pl.when(away)(go)
        else: go()
    def col_wait(sems,x=None):
        @pl.when(away)
        def _():
            wait(colv, NEAR, sems.at[2]); wait(colv, RING-NEAR, sems.at[4])
        wait(colv, NEAR, sems.at[3]); wait(colv, RING-NEAR, sems.at[5])
    col_wait(recv_sem)
    multiply(colv, SLOTS, tiles_t, 0)
    for t in range(OFFS): row_out[t] = acc[last[t]]
    for t in UP:
        @pl.when(k!=t)
        def _(): send(row_out.at[t], row_in.at[k], i, t, 9)
    row_in[k] = row_out[k]
    @pl.when(jnp.logical_not(away))
    def _(): col_in[0] = col_out[0]
    def total(ref, n):
        s = ref[0]
        for t in range(1, n): s = s + ref[t]
        return s
    def wait_col(ref, sem):
        @pl.when(away)
        def _(): wait(ref,OFFS,sem)
        @pl.when(jnp.logical_not(away))
        def _(): wait(ref,OFFS-1,sem)
    wait_col(col_in, recv_sem.at[8])
    cols_sum = total(col_in, OFFS)
    wait(row_in, OFFS-1, recv_sem.at[9])
    out[...] = cols_sum + total(row_in, OFFS)
    wait(rowv, NEAR-1, send_sem.at[0])
    wait(rowv, RING-NEAR, send_sem.at[1])
    wait(rowv, NEAR, send_sem.at[6])
    wait(rowv, RING-NEAR, send_sem.at[7])
    wait(rowv, NEAR, send_sem.at[2]); wait(rowv, RING-NEAR, send_sem.at[4])
    @pl.when(away)
    def _():
        wait(rowv, NEAR, send_sem.at[3]); wait(rowv, RING-NEAR, send_sem.at[5])
    wait_col(col_out, send_sem.at[8])
    wait(row_out, OFFS-1, send_sem.at[9])
def body(vectors, tiles, row_index, col_index, counts):
    nvec, piece = vectors.shape
    block = (nvec, piece)
    hbm = pl.BlockSpec(memory_space=pltpu.MemorySpace.HBM)
    f32=jnp.float32
    return pl.pallas_call(kernel,
        out_shape=pltpu.MemorySpace.VMEM(block, f32),
        in_specs=[hbm] * 5, out_specs=pl.BlockSpec(memory_space=pltpu.VMEM),
        scratch_shapes=[pltpu.VMEM(tiles.shape[2:], tiles.dtype), pltpu.VMEM(tiles.shape[2:], tiles.dtype),
            pltpu.VMEM((OFFS,) + block, vectors.dtype), pltpu.VMEM((OFFS,) + block, vectors.dtype),
            pltpu.VMEM((SLOTS + 1,) + block, f32)] + [pltpu.VMEM((OFFS,) + block, f32)]*4 + [
            pltpu.SMEM((1,1,SLOTS), jnp.int32), pltpu.SMEM((1,1,SLOTS), jnp.int32), pltpu.SMEM((1,1), jnp.int32),
            pltpu.SMEM((2 * SLOTS,), jnp.int32), pltpu.SMEM((2 * OFFS,), jnp.int32), pltpu.SMEM((2 * SLOTS,), jnp.int32),
            pltpu.SemaphoreType.DMA((5,)), pltpu.SemaphoreType.DMA((10,)), pltpu.SemaphoreType.DMA((10,)), pltpu.SemaphoreType.REGULAR],
        compiler_params=pltpu.CompilerParams(collective_id=0, has_side_effects=True, vmem_limit_bytes=60 * 1024 * 1024),
        cost_estimate=pl.CostEstimate(flops=4 * SLOTS * nvec * piece * piece, bytes_accessed=2 * SLOTS * piece * piece, transcendentals=0),
    )(vectors, tiles, row_index, col_index, counts)


def solution(mesh):
    return jax.shard_map(
        body,
        mesh=mesh,
        in_specs=(
            P(None, ("diag", "off")),
            P("diag", "off", None, None, None),
            P("diag", "off", None),
            P("diag", "off", None),
            P("diag", "off"),
        ),
        out_specs=P(None, ("diag", "off")),
        check_vma=False,
    )
```

time: 1770 us -> 44.3 us (0.03)
  waiting for transfers between devices: 1720 us -> 0 us
  Pallas kernels: 0 us -> 42.4 us
  starting transfers between devices: 18.4 us -> 0 us
    all_gather x1 -> x0, waiting for transfers between devices: 1580 us -> none  [body(): everything = lax.all_gather(vectors, ('diag', 'off'), axis=1, tiled=True)]
    reduce_scatter x1 -> x0, waiting for transfers between devices: 115 us -> none  [body(): return lax.psum_scatter(placed, 'diag', scatter_dimension=1, tiled=True)]
    pallas_call x0 -> x1, Pallas kernels: none -> 42.4 us  [body(): pl.pallas_call(kernel, out_shape=pltpu.MemorySpace.VMEM(block, f32), in_s...]
    all_to_all x2 -> x0, waiting for transfers between devices: 25.7 us -> none  [the longest x1 13.4 us: body(): lax.all_to_all(send_cols, 'off', split_axis=0, concat_axis=0, tiled=True)]
    all_to_all x2 -> x0, starting transfers between devices: 18.3 us -> none  [the longest x1 11.7 us: body(): lax.all_to_all(send_rows, 'off', split_axis=0, concat_axis=0, tiled=True)]
  transfers between devices with their start and end apart: 4 -> 0, of which waited for: 4 -> 0; matrix products, arithmetic and copies ran while one was open for 0% -> 0% of each run, Pallas kernels for 0% -> 0%
where the time goes in v2:
time: 44.3 us; the launch traced here: 43.6 us
  Pallas kernels  42.4 us (96%)
  between operations  0.66 us (1%)
  local copies, waits for them, and re-layouts  0.6 us (1%)
    pallas_call x1, Pallas kernels, body(): pl.pallas_call(kernel, out_shape=pltpu.MemorySpace.VMEM(block, f32), in_s...  42.4 us

profile of v2, /device:TPU:6, one launch (start us, length us, event | category | flops | bytes accessed | tf_op | source)
XLA Modules:
  0.0 43.6 jit_solution(380442905872191121)
XLA Ops:
  0.7 42.4 %shard_map.55 = f32[16,128]{1,0:T(8,128)S(1)} custom-call(bf16[16,128]{1,0:T(8,128)(2,1)} %vec_h.1, bf16[1,1,32,128,128]{4,3,2,1,0:T(8,128)(2,1)} %tiles_h.1, s32[1,1,32]{2,1,0:T(1,128)} %row_h.1, s32[1,1,32]{2,1,0:T(1,128)} %col_h.1, s32[1,1]{1,0:T(1,128)S(6)} %copy.8.cnt_h), custom_call_target="tpu_custom_call" | custom-call | flops 33554432 | bytes 1048576 | tf_op jit(solution)/shard_map/pallas_call | solution.py:168
  43.0 0.6 %copy.7 = f32[16,128]{1,0:T(8,128)} copy(f32[16,128]{1,0:T(8,128)S(1)} %shard_map.55) | data formatting | bytes 16384

commit v3 on v0

v3 whole, which is shorter than its diff:
```python
import jax
import jax.numpy as jnp
from jax import lax
from jax.experimental import pallas as pl
from jax.experimental.pallas import tpu as pltpu
from jax.sharding import PartitionSpec as P

MESH = pl.DeviceIdType.MESH
GROUPS, OFFS, RING, SLOTS = 32, 24, 12, 32
PIECES = ((0, 1), (1, 4), (5, 4), (9, 3))
NP = len(PIECES)
LOWC, LOWR = 3, 4
LINE = [6, 5, 7, 4, 8, 3, 9, 2, 10, 1, 11]
def shift(k): return lax.div(k * GROUPS + (OFFS - 1), OFFS)
def slot(d): return 0 if d == 0 else (2 * d - 1 if d <= RING // 2 else 2 * (RING - d))
def kernel(vec_h, tiles_h, row_h, col_h, cnt_h, out,
    tiles, rowv, colv, acc, row_out, col_out, row_in, col_in, row_x, col_x,
    row_s, col_s, cnt_s, table_v, table, in_sem, send_sem, recv_sem, ready):
    i = lax.axis_index("diag"); k = lax.axis_index("off")
    xh = lax.div(k, RING); z = lax.rem(k, RING)
    j = lax.rem(i + shift(k), GROUPS)
    base = xh * RING
    xk = (1 - xh) * RING + z
    away = k != 0
    def user(t): return lax.rem(i - shift(jnp.int32(t)) + GROUPS, GROUPS)
    def line(dz): return base + lax.rem(z + dz, RING)
    barrier = pltpu.get_barrier_semaphore()
    def greet(d, o): pl.semaphore_signal(barrier, inc=1, device_id=(d, o), device_id_type=MESH)
    for dz in LINE[:5]: greet(i, line(dz))
    greet(j, xk)
    @pl.when(away)
    def _(): greet(j, k)
    for dz in LINE[5:]: greet(i, line(dz))
    greet(i, xk)
    loads = [pltpu.make_async_copy(a, b, in_sem.at[n]) for n, (a, b) in enumerate(((vec_h, rowv.at[base]), (row_h, row_s), (col_h, col_s), (cnt_h, cnt_s), (tiles_h.at[0, 0], tiles)))]
    for l in loads: l.start()
    acc[SLOTS] = jnp.zeros(acc.shape[1:], jnp.float32)
    to_smem = pltpu.make_async_copy(table_v, table, in_sem.at[5])
    def prepare():
        for l in loads[1:4]: l.wait()
        live = cnt_s[0, 0]
        lane = lax.broadcasted_iota(jnp.int32, (1, 128), 1)
        for side, ref in enumerate((row_s, col_s)):
            every = jnp.zeros((1, 128), jnp.int32)
            for q in range(SLOTS): every = jnp.where(lane == q, ref[0, 0, q], every)
            before = end = jnp.full((1, 128), SLOTS, jnp.int32)
            for q in range(SLOTS):
                t = ref[0, 0, q]
                before = jnp.where(jnp.logical_and(every == t, lane > q), q, before)
                end = jnp.where(lane == jnp.where(q < live, t, -1), q, end)
            d = every - jnp.where(every >= RING, RING, 0) - z
            d = jnp.where(d < 0, d + RING, d)
            lies = jnp.where(every >= RING, RING, 0) + jnp.where(d == 0, 0, jnp.where(d <= RING // 2, 2 * d - 1, 2 * (RING - d)))
            table_v[pl.ds(side, 1)] = before
            table_v[pl.ds(2 + side, 1)] = end
            table_v[pl.ds(4 + side, 1)] = lies
        to_smem.start()
    loads[0].wait()
    prepare()
    pl.semaphore_wait(barrier, len(LINE) + 2 + jnp.where(away, 1, 0))
    def send(src, dst, d, o, sem, rsem=None):
        pltpu.make_async_remote_copy(src_ref=src, dst_ref=dst, send_sem=send_sem.at[sem], recv_sem=recv_sem.at[sem if rsem is None else rsem], device_id=(d, o), device_id_type=MESH).start()
    def wait(ref, n, sem):
        part = ref.at[pl.ds(0, n)]
        pltpu.make_async_copy(part, part, sem).wait()
    mine = rowv.at[base]
    S_LINE, S_X, S_C = 2, 2 + NP, 2 + 2 * NP
    def piece_of(s): return [n for n, (a, c) in enumerate(PIECES) if a <= s < a + c][0]
    for dz in LINE:
        s = slot((RING - dz) % RING)
        send(mine, rowv.at[base + s], i, line(dz), S_LINE + piece_of(s))
    pl.semaphore_signal(ready, inc=1, device_id=(user(xk), xk), device_id_type=MESH)
    @pl.when(away)
    def _(): pl.semaphore_signal(ready, inc=1, device_id=(user(k), k), device_id_type=MESH)
    for n, (a, c) in enumerate(PIECES):
        got = c - (1 if a == 0 else 0)
        if got: wait(rowv, got, recv_sem.at[S_LINE + n])
        part = pl.ds(base + a, c)
        send(rowv.at[part], colv.at[part], user(xk), xk, S_C + 2 * n, S_C + 2 * n + xh)
        @pl.when(away)
        def _(): send(rowv.at[part], colv.at[part], user(k), k, S_C + 2 * n + 1, S_C + 2 * n + xh)
        send(rowv.at[part], rowv.at[part], i, xk, S_X + n)
    @pl.when(jnp.logical_not(away))
    def _(): colv[pl.ds(base, RING)] = rowv[pl.ds(base, RING)]
    loads[4].wait()
    to_smem.wait()
    def multiply(picked, side, axis):
        for p in range(SLOTS):
            x = picked[table[4 + side, p]]
            y = lax.dot_general(x, tiles[p], (((1,), (axis,)), ((), ())), preferred_element_type=jnp.float32)
            acc[p] = acc[table[1 - side, p]] + y
    for n, (a, c) in enumerate(PIECES): wait(rowv, c, recv_sem.at[S_X + n])
    multiply(rowv, 0, 0)
    pl.semaphore_wait(ready, 1 + jnp.where(away, 1, 0))
    partner = lax.rem(i + GROUPS // 2, GROUPS)
    mine_at = lambda first: pl.ds(base + first, RING - first)
    other_at = lambda first: pl.ds(RING - base + first, RING - first)
    def direct(part, into, d, low, sem, skip):
        for zt in range(low):
            for h in (0, 1):
                t = h * RING + zt
                def go(t=t): send(part.at[t], into.at[k], d, t, sem)
                if skip(t) is None: go()
                else: pl.when(skip(t))(go)
    def paired(part, got, into, d, low, sem, x_sem, skip):
        wait(got, RING - low, recv_sem.at[x_sem])
        here = mine_at(low)
        part[here] = part[here] + got[pl.ds(0, RING - low)]
        for zt in range(low, RING):
            def go(zt=zt): send(part.at[base + zt], into.at[z], d, base + zt, sem)
            if skip(zt) is None: go()
            else: pl.when(skip(zt))(go)
    col_skip = lambda t: away if t == 0 else None
    X_COL, X_ROW = S_C + 2 * NP, S_C + 2 * NP + 1
    for t in range(OFFS): col_out[t] = acc[table[3, t]]
    direct(col_out, col_in, j, LOWC, 0, col_skip)
    if LOWC < RING: send(col_out.at[other_at(LOWC)], col_x.at[pl.ds(0, RING - LOWC)], partner, xk, X_COL)
    def col_wait(sems, swap=False):
        for n, (a, c) in enumerate(PIECES):
            @pl.when(away)
            def _(): wait(colv, c, sems.at[S_C + 2 * n + (1 if swap else 0)])
            wait(colv, c, sems.at[S_C + 2 * n + (0 if swap else 1)])
    col_wait(recv_sem)
    multiply(colv, 1, 1)
    for t in range(OFFS): row_out[t] = acc[table[2, t]]
    direct(row_out, row_in, i, LOWR, 1, lambda t: k != t)
    if LOWR < RING: send(row_out.at[other_at(LOWR)], row_x.at[pl.ds(0, RING - LOWR)], i, xk, X_ROW)
    if LOWC < RING: paired(col_out, col_x, col_in, j, LOWC, 0, X_COL, col_skip)
    if LOWR < RING: paired(row_out, row_x, row_in, i, LOWR, 1, X_ROW, lambda zt: z != zt)
    row_in[jnp.where(z < LOWR, k, z)] = row_out[k]
    @pl.when(jnp.logical_not(away))
    def _(): col_in[0] = col_out[0]
    def total(ref, n):
        s = ref[0]
        for t in range(1, n): s = s + ref[t]
        return s
    def finish(ref, low, sem, first):
        def some(n, when):
            @pl.when(when)
            def _():
                if first:
                    @pl.when(away)
                    def _(): wait(ref, n, sem)
                    @pl.when(jnp.logical_not(away))
                    def _(): wait(ref, n - 1, sem)
                    out[...] = total(ref, n)
                else:
                    wait(ref, n - 1, sem)
                    out[...] = out[...] + total(ref, n)
        if low > 0: some(OFFS, z < low)
        if low < RING: some(RING, z >= low)
    finish(col_in, LOWC, recv_sem.at[0], True)
    finish(row_in, LOWR, recv_sem.at[1], False)
    n_col = 2 * LOWC + RING - LOWC; n_row = 2 * LOWR + RING - LOWR - 1
    @pl.when(away)
    def _(): wait(col_out, n_col, send_sem.at[0])
    @pl.when(jnp.logical_not(away))
    def _(): wait(col_out, n_col - 1, send_sem.at[0])
    wait(row_out, n_row, send_sem.at[1])
    if LOWC < RING: wait(col_x, RING - LOWC, send_sem.at[X_COL])
    if LOWR < RING: wait(row_x, RING - LOWR, send_sem.at[X_ROW])
    for n, (a, c) in enumerate(PIECES):
        got = c - (1 if a == 0 else 0)
        if got: wait(rowv, got, send_sem.at[S_LINE + n])
        wait(rowv, c, send_sem.at[S_X + n])
    col_wait(send_sem, True)
def body(vectors, tiles, row_index, col_index, counts):
    nvec, piece = vectors.shape
    block = (nvec, piece)
    hbm = pl.BlockSpec(memory_space=pltpu.MemorySpace.HBM)
    f32 = jnp.float32
    n_sems = 4 + 4 * NP
    return pl.pallas_call(kernel,
        out_shape=pltpu.MemorySpace.VMEM(block, f32),
        in_specs=[hbm] * 5, out_specs=pl.BlockSpec(memory_space=pltpu.VMEM),
        scratch_shapes=[pltpu.VMEM(tiles.shape[2:], tiles.dtype),
            pltpu.VMEM((OFFS,) + block, vectors.dtype), pltpu.VMEM((OFFS,) + block, vectors.dtype),
            pltpu.VMEM((SLOTS + 1,) + block, f32)] + [pltpu.VMEM((OFFS,) + block, f32)]*4 + [pltpu.VMEM((RING,) + block, f32)]*2 + [
            pltpu.SMEM((1, 1, SLOTS), jnp.int32), pltpu.SMEM((1, 1, SLOTS), jnp.int32), pltpu.SMEM((1, 1), jnp.int32),
            pltpu.VMEM((8, 128), jnp.int32), pltpu.SMEM((8, 128), jnp.int32),
            pltpu.SemaphoreType.DMA((6,)), pltpu.SemaphoreType.DMA((n_sems,)), pltpu.SemaphoreType.DMA((n_sems,)), pltpu.SemaphoreType.REGULAR],
        compiler_params=pltpu.CompilerParams(collective_id=0, has_side_effects=True, vmem_limit_bytes=60 * 1024 * 1024),
        cost_estimate=pl.CostEstimate(flops=4 * SLOTS * nvec * piece * piece, bytes_accessed=2 * SLOTS * piece * piece, transcendentals=0),
    )(vectors, tiles, row_index, col_index, counts)


def solution(mesh):
    return jax.shard_map(
        body,
        mesh=mesh,
        in_specs=(
            P(None, ("diag", "off")),
            P("diag", "off", None, None, None),
            P("diag", "off", None),
            P("diag", "off", None),
            P("diag", "off"),
        ),
        out_specs=P(None, ("diag", "off")),
        check_vma=False,
    )
```

time: 1770 us -> 41 us (0.02)
  waiting for transfers between devices: 1720 us -> 0 us
  Pallas kernels: 0 us -> 39.2 us
  starting transfers between devices: 18.4 us -> 0 us
    all_gather x1 -> x0, waiting for transfers between devices: 1580 us -> none  [body(): everything = lax.all_gather(vectors, ('diag', 'off'), axis=1, tiled=True)]
    reduce_scatter x1 -> x0, waiting for transfers between devices: 115 us -> none  [body(): return lax.psum_scatter(placed, 'diag', scatter_dimension=1, tiled=True)]
    pallas_call x0 -> x1, Pallas kernels: none -> 39.2 us  [body(): pl.pallas_call(kernel, out_shape=pltpu.MemorySpace.VMEM(block, f32), in_s...]
    all_to_all x2 -> x0, waiting for transfers between devices: 25.7 us -> none  [the longest x1 13.4 us: body(): lax.all_to_all(send_cols, 'off', split_axis=0, concat_axis=0, tiled=True)]
    all_to_all x2 -> x0, starting transfers between devices: 18.3 us -> none  [the longest x1 11.7 us: body(): lax.all_to_all(send_rows, 'off', split_axis=0, concat_axis=0, tiled=True)]
  transfers between devices with their start and end apart: 4 -> 0, of which waited for: 4 -> 0; matrix products, arithmetic and copies ran while one was open for 0% -> 0% of each run, Pallas kernels for 0% -> 0%
where the time goes in v3:
time: 41 us; the launch traced here: 40.5 us
  Pallas kernels  39.2 us (96%)
  between operations  0.66 us (2%)
  local copies, waits for them, and re-layouts  0.6 us (1%)
    pallas_call x1, Pallas kernels, body(): pl.pallas_call(kernel, out_shape=pltpu.MemorySpace.VMEM(block, f32), in_s...  39.2 us

profile of v3, /device:TPU:6, one launch (start us, length us, event | category | flops | bytes accessed | tf_op | source)
XLA Modules:
  0.0 40.5 jit_solution(5553911719169177827)
XLA Ops:
  0.7 39.2 %shard_map.55 = f32[16,128]{1,0:T(8,128)S(1)} custom-call(bf16[16,128]{1,0:T(8,128)(2,1)} %vec_h.1, bf16[1,1,32,128,128]{4,3,2,1,0:T(8,128)(2,1)} %tiles_h.1, s32[1,1,32]{2,1,0:T(1,128)} %row_h.1, s32[1,1,32]{2,1,0:T(1,128)} %col_h.1, s32[1,1]{1,0:T(1,128)S(6)} %copy.8.cnt_h), custom_call_target="tpu_custom_call" | custom-call | flops 33554432 | bytes 1048576 | tf_op jit(solution)/shard_map/pallas_call | solution.py:173
  39.9 0.6 %copy.7 = f32[16,128]{1,0:T(8,128)} copy(f32[16,128]{1,0:T(8,128)S(1)} %shard_map.55) | data formatting | bytes 16384

commit v4 on v3

--- a/solution.py
+++ b/solution.py
@@ -9,6 +9,8 @@
 GROUPS, OFFS, RING, SLOTS = 32, 24, 12, 32
 PIECES = ((0, 1), (1, 4), (5, 4), (9, 3))
 NP = len(PIECES)
+NEAR_UP, NEAR_DOWN = 3, 3
+NEAR = [q for q in range(RING) if q < NEAR_UP or q >= RING - NEAR_DOWN]
 LOWC, LOWR = 3, 4
 LINE = [6, 5, 7, 4, 8, 3, 9, 2, 10, 1, 11]
 def shift(k): return lax.div(k * GROUPS + (OFFS - 1), OFFS)
@@ -22,6 +24,10 @@
     base = xh * RING
     xk = (1 - xh) * RING + z
     away = k != 0
+    near = jnp.logical_or(z < NEAR_UP, z >= RING - NEAR_DOWN)
+    def either(go):
+        pl.when(near)(lambda: go(0, 0))
+        pl.when(jnp.logical_not(near))(lambda: go(LOWC, LOWR))
     def user(t): return lax.rem(i - shift(jnp.int32(t)) + GROUPS, GROUPS)
     def line(dz): return base + lax.rem(z + dz, RING)
     barrier = pltpu.get_barrier_semaphore()
@@ -113,8 +119,10 @@
     col_skip = lambda t: away if t == 0 else None
     X_COL, X_ROW = S_C + 2 * NP, S_C + 2 * NP + 1
     for t in range(OFFS): col_out[t] = acc[table[3, t]]
-    direct(col_out, col_in, j, LOWC, 0, col_skip)
-    if LOWC < RING: send(col_out.at[other_at(LOWC)], col_x.at[pl.ds(0, RING - LOWC)], partner, xk, X_COL)
+    def col_first(low, _):
+        direct(col_out, col_in, j, low, 0, col_skip)
+        send(col_out.at[other_at(low)], col_x.at[pl.ds(0, RING - low)], partner, xk, X_COL)
+    either(col_first)
     def col_wait(sems, swap=False):
         for n, (a, c) in enumerate(PIECES):
             @pl.when(away)
@@ -123,16 +131,19 @@
     col_wait(recv_sem)
     multiply(colv, 1, 1)
     for t in range(OFFS): row_out[t] = acc[table[2, t]]
-    direct(row_out, row_in, i, LOWR, 1, lambda t: k != t)
-    if LOWR < RING: send(row_out.at[other_at(LOWR)], row_x.at[pl.ds(0, RING - LOWR)], i, xk, X_ROW)
-    if LOWC < RING: paired(col_out, col_x, col_in, j, LOWC, 0, X_COL, col_skip)
-    if LOWR < RING: paired(row_out, row_x, row_in, i, LOWR, 1, X_ROW, lambda zt: z != zt)
-    row_in[jnp.where(z < LOWR, k, z)] = row_out[k]
+    def row_first(lowc, low):
+        direct(row_out, row_in, i, low, 1, lambda t: k != t)
+        send(row_out.at[other_at(low)], row_x.at[pl.ds(0, RING - low)], i, xk, X_ROW)
+        paired(col_out, col_x, col_in, j, lowc, 0, X_COL, col_skip)
+        paired(row_out, row_x, row_in, i, low, 1, X_ROW, lambda zt: z != zt)
+    either(row_first)
+    row_in[jnp.where(jnp.logical_and(z < LOWR, jnp.logical_not(near)), k, z)] = row_out[k]
     @pl.when(jnp.logical_not(away))
     def _(): col_in[0] = col_out[0]
     def total(ref, n):
-        s = ref[0]
-        for t in range(1, n): s = s + ref[t]
+        used = [q for q in range(OFFS) if q < RING or (n > RING and q - RING not in NEAR)]
+        s = ref[used[0]]
+        for q in used[1:]: s = s + ref[q]
         return s
     def finish(ref, low, sem, first):
         def some(n, when):
@@ -147,18 +158,20 @@
                 else:
                     wait(ref, n - 1, sem)
                     out[...] = out[...] + total(ref, n)
-        if low > 0: some(OFFS, z < low)
+        if low > 0: some(OFFS - len(NEAR), z < low)
         if low < RING: some(RING, z >= low)
     finish(col_in, LOWC, recv_sem.at[0], True)
     finish(row_in, LOWR, recv_sem.at[1], False)
-    n_col = 2 * LOWC + RING - LOWC; n_row = 2 * LOWR + RING - LOWR - 1
-    @pl.when(away)
-    def _(): wait(col_out, n_col, send_sem.at[0])
-    @pl.when(jnp.logical_not(away))
-    def _(): wait(col_out, n_col - 1, send_sem.at[0])
-    wait(row_out, n_row, send_sem.at[1])
-    if LOWC < RING: wait(col_x, RING - LOWC, send_sem.at[X_COL])
-    if LOWR < RING: wait(row_x, RING - LOWR, send_sem.at[X_ROW])
+    def sent(lowc, lowr):
+        n_col = lowc + RING
+        @pl.when(away)
+        def _(): wait(col_out, n_col, send_sem.at[0])
+        @pl.when(jnp.logical_not(away))
+        def _(): wait(col_out, n_col - 1, send_sem.at[0])
+        wait(row_out, lowr + RING - 1, send_sem.at[1])
+        wait(col_x, RING - lowc, send_sem.at[X_COL])
+        wait(row_x, RING - lowr, send_sem.at[X_ROW])
+    either(sent)
     for n, (a, c) in enumerate(PIECES):
         got = c - (1 if a == 0 else 0)
         if got: wait(rowv, got, send_sem.at[S_LINE + n])

time: 41 us -> 41.2 us (level)
  Pallas kernels: 39.2 us -> 39.8 us
    pallas_call x1, Pallas kernels: 39.2 us -> 39.8 us  [body(): pl.pallas_call(kernel, out_shape=pltpu.MemorySpace.VMEM(block, f32), in_s...]
where the time goes in v4:
time: 41.2 us; the launch traced here: 41.1 us
  Pallas kernels  39.8 us (97%)
  between operations  0.66 us (2%)
  local copies, waits for them, and re-layouts  0.6 us (1%)
    pallas_call x1, Pallas kernels, body(): pl.pallas_call(kernel, out_shape=pltpu.MemorySpace.VMEM(block, f32), in_s...  39.8 us

profile of v4, /device:TPU:6, one launch (start us, length us, event | category | flops | bytes accessed | tf_op | source)
XLA Modules:
  0.0 41.1 jit_solution(15280037073938603108)
XLA Ops:
  0.7 39.8 %shard_map.55 = f32[16,128]{1,0:T(8,128)S(1)} custom-call(bf16[16,128]{1,0:T(8,128)(2,1)} %vec_h.1, bf16[1,1,32,128,128]{4,3,2,1,0:T(8,128)(2,1)} %tiles_h.1, s32[1,1,32]{2,1,0:T(1,128)} %row_h.1, s32[1,1,32]{2,1,0:T(1,128)} %col_h.1, s32[1,1]{1,0:T(1,128)S(6)} %copy.8.cnt_h), custom_call_target="tpu_custom_call" | custom-call | flops 33554432 | bytes 1048576 | tf_op jit(solution)/shard_map/pallas_call | solution.py:186
  40.5 0.6 %copy.7 = f32[16,128]{1,0:T(8,128)} copy(f32[16,128]{1,0:T(8,128)S(1)} %shard_map.55) | data formatting | bytes 16384

commit v5 on v4

--- a/solution.py
+++ b/solution.py
@@ -9,7 +9,7 @@
 GROUPS, OFFS, RING, SLOTS = 32, 24, 12, 32
 PIECES = ((0, 1), (1, 4), (5, 4), (9, 3))
 NP = len(PIECES)
-NEAR_UP, NEAR_DOWN = 3, 3
+NEAR_UP, NEAR_DOWN = 1, 1
 NEAR = [q for q in range(RING) if q < NEAR_UP or q >= RING - NEAR_DOWN]
 LOWC, LOWR = 3, 4
 LINE = [6, 5, 7, 4, 8, 3, 9, 2, 10, 1, 11]

time: 41.2 us -> 40.9 us (level)
  no operation moved by 1% of the time
where the time goes in v5:
time: 40.9 us; the launch traced here: 40.7 us
  Pallas kernels  39.4 us (96%)
  between operations  0.66 us (2%)
  local copies, waits for them, and re-layouts  0.6 us (1%)
    pallas_call x1, Pallas kernels, body(): pl.pallas_call(kernel, out_shape=pltpu.MemorySpace.VMEM(block, f32), in_s...  39.4 us

profile of v5, /device:TPU:6, one launch (start us, length us, event | category | flops | bytes accessed | tf_op | source)
XLA Modules:
  0.0 40.7 jit_solution(9890505846386767500)
XLA Ops:
  0.7 39.4 %shard_map.55 = f32[16,128]{1,0:T(8,128)S(1)} custom-call(bf16[16,128]{1,0:T(8,128)(2,1)} %vec_h.1, bf16[1,1,32,128,128]{4,3,2,1,0:T(8,128)(2,1)} %tiles_h.1, s32[1,1,32]{2,1,0:T(1,128)} %row_h.1, s32[1,1,32]{2,1,0:T(1,128)} %col_h.1, s32[1,1]{1,0:T(1,128)S(6)} %copy.8.cnt_h), custom_call_target="tpu_custom_call" | custom-call | flops 33554432 | bytes 1048576 | tf_op jit(solution)/shard_map/pallas_call | solution.py:186
  40.1 0.6 %copy.7 = f32[16,128]{1,0:T(8,128)} copy(f32[16,128]{1,0:T(8,128)S(1)} %shard_map.55) | data formatting | bytes 16384
